TPU v7x, 256 devices: a whole 4x4x8 slice. The times are simulated.
256 devices in a mesh: slab: 32 (over z_lo, y, core), tm: 8 (over x, z_hi).
Axes of the slice: x: 4, y: 4, z: 8 (z_hi: 2, z_lo: 4; z = z_hi * 4 + z_lo), core: 2. Of those that a mesh axis runs over, the one named last changes fastest.
Arguments:
- recording: bfloat16 [512, 65536], P('tm', 'slab'), may hold values from -6 to 6
- footprints: bfloat16 [2176, 8192], P(None, 'slab'), may hold values from -0.125 to 0.125
- traces: float32 [512, 8192], P('tm', 'slab'), may hold values from 0 to 2
- live_count: int32 [32], replicated, may hold values from 1 to 256, 6144 in all
Outputs:
- new_traces: float32 [512, 8192], P('tm', 'slab')
- new_footprints: bfloat16 [2176, 8192], P('tm', 'slab')
Inputs may be any that keep to these rules, and one draw needn't show every extreme that they name: Slots 0 .. live_count[s] - 1 of slab s are live; some slab has all 256 live.
All inputs are finite; a program needn't handle non-finite values.
Results may differ from a plain program's by a relative error of at most 0.0034.
Values may be sent and summed in bfloat16 or wider, within the bound.
A program may use at most 64 MiB of HBM per device.

v0:
```python
import jax
import jax.numpy as jnp
from jax import lax
from jax.sharding import PartitionSpec as P

GROUP = 128
GROUPS_DEV = 2


def passed_along(block, axis, distance):
    devices = range(lax.axis_size(axis))
    route = [(i - distance, i) for i in devices if i - distance in devices]
    return lax.ppermute(block, axis, route)


def with_halo(cells, sides, width):
    for axis, dim in sides:
        count = lax.axis_size(axis)
        ends = count - 1
        head = lax.slice_in_dim(cells, 0, width, axis=dim)
        tail = lax.slice_in_dim(cells, cells.shape[dim] - width, cells.shape[dim], axis=dim)
        cells = jnp.concatenate(
            [
                lax.ppermute(tail, axis, [(i, (i + 1) % count) for i in range(ends)]),
                cells,
                lax.ppermute(head, axis, [((i + 1) % count, i) for i in range(ends)]),
            ],
            axis=dim,
        )
    return cells


def contract_first(left, right):
    return lax.dot_general(
        left, right, (((0,), (0,)), ((), ())), preferred_element_type=jnp.float32
    )


def on_device(recording, footprints, traces, live_count):
    slabs = lax.axis_size("slab")
    slab_index = lax.axis_index("slab")
    neurons = traces.shape[1]
    extended = footprints.shape[0]
    voxels = recording.shape[1]
    rim_rows = extended - voxels
    slots = jnp.arange(neurons, dtype=jnp.int32)
    live_here = jnp.sum(jnp.where(jnp.arange(slabs, dtype=jnp.int32) == slab_index, live_count, 0))
    living = slots < live_here
    row_ids = jnp.arange(extended, dtype=jnp.int32)
    kept_mask = living[None, :] & ((row_ids[:, None] < voxels) | (slab_index < slabs - 1))
    masked_foot = jnp.where(kept_mask, footprints, jnp.zeros_like(footprints))
    start_tr = jnp.where(living[None, :], traces, jnp.zeros_like(traces))
    next_edge, movie_rim = passed_along(
        (masked_foot[:rim_rows], recording[:, :rim_rows]), "slab", -1
    )
    prev_rim = passed_along(masked_foot[voxels:], "slab", 1)
    movie_ext = jnp.concatenate([recording, movie_rim], 1)
    drive = jnp.dot(movie_ext, masked_foot, preferred_element_type=jnp.float32)
    gram_own = contract_first(masked_foot, masked_foot)
    gram_prev = contract_first(masked_foot[:rim_rows], prev_rim)
    gram_next = contract_first(masked_foot[voxels:], next_edge)
    diag_own = jnp.diagonal(gram_own) + 1e-06
    halo_tr = with_halo(start_tr, (("slab", 1),), neurons)
    prev_c = halo_tr[:, :neurons]
    next_c = halo_tr[:, 2 * neurons :]
    outside = jnp.dot(prev_c, gram_prev.T, precision=lax.Precision.HIGHEST) + jnp.dot(
        next_c, gram_next.T, precision=lax.Precision.HIGHEST
    )

    def sweep(group_id, current):
        offset = group_id * GROUP
        columns = lax.dynamic_slice_in_dim(gram_own, offset, GROUP, 1)
        coupled = jnp.dot(
            current, columns, precision=lax.Precision.HIGHEST
        ) + lax.dynamic_slice_in_dim(outside, offset, GROUP, 1)
        before = lax.dynamic_slice_in_dim(current, offset, GROUP, 1)
        driven = lax.dynamic_slice_in_dim(drive, offset, GROUP, 1)
        scaled = lax.dynamic_slice_in_dim(diag_own, offset, GROUP, 0)
        updated = jnp.maximum(before + (driven - coupled) / scaled, 0.0)
        return lax.dynamic_update_slice_in_dim(current, updated, offset, 1)

    new_tr = lax.fori_loop(0, GROUPS_DEV, sweep, start_tr)
    rounded = new_tr.astype(jnp.bfloat16)
    side_tr = with_halo(rounded, (("slab", 1),), neurons)
    frames_all = lax.all_gather(side_tr, "tm", axis=0, tiled=True)
    prev_all = frames_all[:, :neurons]
    own_all = frames_all[:, neurons : 2 * neurons]
    next_all = frames_all[:, 2 * neurons :]
    q_own = contract_first(own_all, own_all)
    q_prev = contract_first(prev_all, own_all)
    q_next = contract_first(next_all, own_all)
    divisor = jnp.maximum(jnp.diagonal(q_own), 1.0)
    share_rows = extended // lax.axis_size("tm")
    first_row = lax.axis_index("tm") * share_rows
    blocks = lax.all_to_all(movie_ext, "tm", split_axis=1, concat_axis=0, tiled=True)
    proj_rows = contract_first(blocks, own_all)
    zero_rows = jnp.zeros((voxels, neurons), jnp.bfloat16)
    prev_full = jnp.concatenate([prev_rim, zero_rows], 0)
    next_full = jnp.concatenate([zero_rows, next_edge], 0)
    foot_share = lax.dynamic_slice_in_dim(masked_foot, first_row, share_rows, 0).astype(jnp.float32)
    prev_share = lax.dynamic_slice_in_dim(prev_full, first_row, share_rows, 0).astype(jnp.float32)
    next_share = lax.dynamic_slice_in_dim(next_full, first_row, share_rows, 0).astype(jnp.float32)
    coupling = jnp.dot(foot_share, q_own, precision=lax.Precision.HIGHEST)
    coupling = coupling + jnp.dot(prev_share, q_prev, precision=lax.Precision.HIGHEST)
    coupling = coupling + jnp.dot(next_share, q_next, precision=lax.Precision.HIGHEST)
    new_foot = jnp.maximum(foot_share + (proj_rows - coupling) / divisor, 0.0).astype(jnp.bfloat16)
    return (new_tr, new_foot)


def solution(mesh):
    placed = (P("tm", "slab"), P(None, "slab"), P("tm", "slab"), P())
    return jax.shard_map(
        on_device,
        mesh=mesh,
        in_specs=placed,
        out_specs=(P("tm", "slab"), P("tm", "slab")),
        check_vma=False,
    )
```

profile of v0, /device:TPU:32, one launch (start us, length us, event | category | flops | bytes accessed | tf_op | source)
XLA Modules:
  0.0 112.4 jit_solution(6685149426623411708)
XLA Ops:
  0.6 1.3 %fusion.26 = s32[]{:T(128)} fusion(s32[32]{0:T(128)} %param.9, s32[]{:T(128)S(6)} %axis_index.23), kind=kLoop, calls=%fused_computation.45 | loop fusion | flops 95 | bytes 136 | tf_op jit(solution)/shard_map/reduce_sum | solution.py:47
  1.9 0.6 iota_compare_fusion.1
  2.6 0.8 broadcast_select_fusion
  3.4 3.9 %collective-permute-start.3 = (f32[64,256]{1,0:T(8,128)S(1)}, f32[64,256]{1,0:T(8,128)S(1)}, u32[]{:S(2)}, u32[]{:S(2)}) collective-permute-start(f32[64,256]{1,0:T(8,128)S(1)} %broadcast_select_fusion), channel_id=1, source_target_pairs={{8,0},{16,8},{24,16},{32,24},{40,32},{48,40},{56,48},{64,56},{72,6... | collective-permute-start | bytes 196616 | tf_op jit(solution)/shard_map/ppermute | solution.py:26
  7.3 1.9 %collective-permute-start.1 = (f32[64,256]{1,0:T(8,128)S(1)}, f32[64,256]{1,0:T(8,128)S(1)}, u32[]{:S(2)}, u32[]{:S(2)}) collective-permute-start(f32[64,256]{1,0:T(8,128)S(1)} %broadcast_select_fusion), channel_id=1, source_target_pairs={{0,8},{8,16},{16,24},{24,32},{32,40},{40,48},{48,56},{56,64},{64,7... | collective-permute-start | bytes 196616 | tf_op jit(solution)/shard_map/ppermute | solution.py:24
  9.3 0.0 copy-start.1
  9.3 2.3 %and_select_fusion = bf16[2176,256]{1,0:T(8,128)(2,1)S(1)} fusion(bf16[2176,256]{1,0:T(8,128)(2,1)} %param.7, pred[256]{0:T(512)(128)(4,1)S(1)} %iota_compare_fusion.1, pred[2176]{0:T(1024)(128)(4,1)S(1)} %fusion.22), kind=kLoop, calls=%fused_computation.11 | loop fusion | flops 1114112 | bytes 2230656 | tf_op jit(solution)/shard_map/jit(_where)/select_n | solution.py:51
  11.6 5.8 %collective-permute-start.4 = (bf16[128,256]{1,0:T(8,128)(2,1)S(1)}, bf16[128,256]{1,0:T(8,128)(2,1)S(1)}, u32[]{:S(2)}, u32[]{:S(2)}) collective-permute-start(bf16[128,256]{1,0:T(8,128)(2,1)S(1)} %get-tuple-element.125), channel_id=1, source_target_pairs={{8,0},{16,8},{24,16},{32,24},{40,32},{48,40},{56,48},{64,56},{72,6... | collective-permute-start | bytes 196616 | tf_op jit(solution)/shard_map/ppermute | solution.py:13
  17.3 1.9 %collective-permute-start.2 = (bf16[128,256]{1,0:T(8,128)(2,1)S(1)}, bf16[128,256]{1,0:T(8,128)(2,1)S(1)}, u32[]{:S(2)}, u32[]{:S(2)}) collective-permute-start(bf16[128,256]{1,0:T(8,128)(2,1)S(1)} %get-tuple-element.124), channel_id=1, source_target_pairs={{0,8},{8,16},{16,24},{24,32},{32,40},{40,48},{48,56},{56,64},{64,7... | collective-permute-start | bytes 196616 | tf_op jit(solution)/shard_map/ppermute | solution.py:13
  19.3 0.0 copy-done.1
  19.3 5.8 %collective-permute-start = (bf16[64,128]{1,0:T(8,128)(2,1)S(1)}, bf16[64,128]{1,0:T(8,128)(2,1)S(1)}, u32[]{:S(2)}, u32[]{:S(2)}) collective-permute-start(bf16[64,128]{1,0:T(8,128)(2,1)S(1)} %slice.20), channel_id=1, source_target_pairs={{8,0},{16,8},{24,16},{32,24},{40,32},{48,40},{56,48},{64,56},{72,6... | collective-permute-start | bytes 49160 | tf_op jit(solution)/shard_map/ppermute | solution.py:13
  25.1 0.5 fusion.35
  25.6 2.3 %gather_fusion = f32[256]{0:T(256)S(1)} fusion(f32[256,256]{1,0:T(8,128)S(1)} %fusion.35, s32[256]{0:T(256)S(1)} %bitcast.35), kind=kCustom, calls=%fused_computation | custom fusion | bytes 4096 | tf_op jit(solution)/shard_map/jit(diagonal)/cond/branch_0_fun/gather | solution.py:62
  28.0 0.0 collective-permute-done
  28.0 0.3 fusion.34
  28.3 0.0 collective-permute-done.4
  28.3 0.2 fusion.29
  28.5 0.0 collective-permute-done.2
  28.5 0.2 fusion.31
  28.8 0.0 collective-permute-done.3
  28.8 0.4 fusion.36
  29.1 0.0 collective-permute-done.1
  29.1 0.4 convolution_add_fusion.2
  29.5 0.7 while.13
  29.5 0.1 dynamic_slice.68
  29.6 0.2 fusion.57
  29.9 0.1 dynamic_slice.68
  29.9 0.2 fusion.57
  30.2 0.0 copy-start
  30.2 1.9 %collective-permute-start.5 = (bf16[64,256]{1,0:T(8,128)(2,1)S(1)}, bf16[64,256]{1,0:T(8,128)(2,1)S(1)}, u32[]{:S(2)}, u32[]{:S(2)}) collective-permute-start(bf16[64,256]{1,0:T(8,128)(2,1)S(1)} %convert_element_type.12), channel_id=1, source_target_pairs={{0,8},{8,16},{16,24},{24,32},{32,40},{40,48},{48,56},{56,64},{64,7... | collective-permute-start | bytes 98312 | tf_op jit(solution)/shard_map/ppermute | solution.py:24
  32.2 5.8 %collective-permute-start.6 = (bf16[64,256]{1,0:T(8,128)(2,1)S(1)}, bf16[64,256]{1,0:T(8,128)(2,1)S(1)}, u32[]{:S(2)}, u32[]{:S(2)}) collective-permute-start(bf16[64,256]{1,0:T(8,128)(2,1)S(1)} %convert_element_type.12), channel_id=1, source_target_pairs={{8,0},{16,8},{24,16},{32,24},{40,32},{48,40},{56,48},{64,56},{72,6... | collective-permute-start | bytes 98312 | tf_op jit(solution)/shard_map/ppermute | solution.py:26
  37.9 0.5 all_to_all.14
  38.4 0.8 copy.6
  39.2 0.0 copy-done
  39.2 10.9 %all-to-all-start = ((bf16[64,8,272]{2,0,1:T(8,128)(2,1)}), bf16[64,8,272]{2,0,1:T(8,128)(2,1)S(1)}, u32[]{:S(2)}, u32[]{:S(2)}) async-start(bf16[64,8,272]{2,0,1:T(8,128)(2,1)} %copy.6), calls=%async_computation | async-start | bytes 786432 | tf_op jit(solution)/shard_map/all_to_all | solution.py:95
  50.1 0.0 collective-permute-done.5
  50.1 0.0 collective-permute-done.6
  50.2 57.1 %all_gather.3 = bf16[512,768]{1,0:T(8,128)(2,1)S(1)} all-gather(bf16[64,768]{1,0:T(8,128)(2,1)S(1)} %pad_maximum_fusion), channel_id=1, replica_groups=mesh['slab'=32,'tm'=8] {'tm'}, dimensions={0}, use_global_device_ids=true | all-gather | bytes 884736 | tf_op jit(solution)/shard_map/all_gather | solution.py:85
  107.3 0.3 fusion.17
  107.5 0.3 fusion.13
  107.8 2.3 %gather_fusion.1 = f32[256]{0:T(256)S(1)} fusion(f32[256,256]{1,0:T(8,128)S(1)} %fusion.17, s32[256]{0:T(256)S(1)} %bitcast.36), kind=kCustom, calls=%fused_computation.1 | custom fusion | bytes 4096 | tf_op jit(solution)/shard_map/jit(diagonal)/cond/branch_0_fun/gather | solution.py:92
  110.1 0.3 fusion.20
  110.5 0.3 convolution_add_fusion.1
  110.8 0.3 fusion.11
  111.1 0.4 convolution_add_fusion
  111.4 0.0 all-to-all-done
  111.4 0.9 fusion.10
  (12 shorter events, 0.1 us)
Async XLA Ops:
  3.4 25.3 %collective-permute-start.3 = (f32[64,256]{1,0:T(8,128)S(1)}, f32[64,256]{1,0:T(8,128)S(1)}, u32[]{:S(2)}, u32[]{:S(2)}) collective-permute-start(f32[64,256]{1,0:T(8,128)S(1)} %broadcast_select_fusion), channel_id=1, source_target_pairs={{8,0},{16,8},{24,16},{32,24},{40,32},{48,40},{56,48},{64,56},{72,6... | collective-permute-start | bytes 196616 | tf_op jit(solution)/shard_map/ppermute | solution.py:26
  7.3 21.8 %collective-permute-start.1 = (f32[64,256]{1,0:T(8,128)S(1)}, f32[64,256]{1,0:T(8,128)S(1)}, u32[]{:S(2)}, u32[]{:S(2)}) collective-permute-start(f32[64,256]{1,0:T(8,128)S(1)} %broadcast_select_fusion), channel_id=1, source_target_pairs={{0,8},{8,16},{16,24},{24,32},{32,40},{40,48},{48,56},{56,64},{64,7... | collective-permute-start | bytes 196616 | tf_op jit(solution)/shard_map/ppermute | solution.py:24
  9.3 10.0 %copy-start.1 = (bf16[64,2048]{1,0:T(8,128)(2,1)S(1)}, bf16[64,2048]{1,0:T(8,128)(2,1)}, u32[]{:S(2)}) copy-start(bf16[64,2048]{1,0:T(8,128)(2,1)} %param.6) | copy-start | bytes 786436
  11.6 16.7 %collective-permute-start.4 = (bf16[128,256]{1,0:T(8,128)(2,1)S(1)}, bf16[128,256]{1,0:T(8,128)(2,1)S(1)}, u32[]{:S(2)}, u32[]{:S(2)}) collective-permute-start(bf16[128,256]{1,0:T(8,128)(2,1)S(1)} %get-tuple-element.125), channel_id=1, source_target_pairs={{8,0},{16,8},{24,16},{32,24},{40,32},{48,40},{56,48},{64,56},{72,6... | collective-permute-start | bytes 196616 | tf_op jit(solution)/shard_map/ppermute | solution.py:13
  17.3 11.2 %collective-permute-start.2 = (bf16[128,256]{1,0:T(8,128)(2,1)S(1)}, bf16[128,256]{1,0:T(8,128)(2,1)S(1)}, u32[]{:S(2)}, u32[]{:S(2)}) collective-permute-start(bf16[128,256]{1,0:T(8,128)(2,1)S(1)} %get-tuple-element.124), channel_id=1, source_target_pairs={{0,8},{8,16},{16,24},{24,32},{32,40},{40,48},{48,56},{56,64},{64,7... | collective-permute-start | bytes 196616 | tf_op jit(solution)/shard_map/ppermute | solution.py:13
  19.3 8.7 %collective-permute-start = (bf16[64,128]{1,0:T(8,128)(2,1)S(1)}, bf16[64,128]{1,0:T(8,128)(2,1)S(1)}, u32[]{:S(2)}, u32[]{:S(2)}) collective-permute-start(bf16[64,128]{1,0:T(8,128)(2,1)S(1)} %slice.20), channel_id=1, source_target_pairs={{8,0},{16,8},{24,16},{32,24},{40,32},{48,40},{56,48},{64,56},{72,6... | collective-permute-start | bytes 49160 | tf_op jit(solution)/shard_map/ppermute | solution.py:13
  30.2 9.0 %copy-start = (f32[64,256]{1,0:T(8,128)}, f32[64,256]{1,0:T(8,128)S(1)}, u32[]{:S(2)}) copy-start(f32[64,256]{1,0:T(8,128)S(1)} %get-tuple-element.109) | copy-start | bytes 196612
  30.2 19.9 %collective-permute-start.5 = (bf16[64,256]{1,0:T(8,128)(2,1)S(1)}, bf16[64,256]{1,0:T(8,128)(2,1)S(1)}, u32[]{:S(2)}, u32[]{:S(2)}) collective-permute-start(bf16[64,256]{1,0:T(8,128)(2,1)S(1)} %convert_element_type.12), channel_id=1, source_target_pairs={{0,8},{8,16},{16,24},{24,32},{32,40},{40,48},{48,56},{56,64},{64,7... | collective-permute-start | bytes 98312 | tf_op jit(solution)/shard_map/ppermute | solution.py:24
  32.2 18.0 %collective-permute-start.6 = (bf16[64,256]{1,0:T(8,128)(2,1)S(1)}, bf16[64,256]{1,0:T(8,128)(2,1)S(1)}, u32[]{:S(2)}, u32[]{:S(2)}) collective-permute-start(bf16[64,256]{1,0:T(8,128)(2,1)S(1)} %convert_element_type.12), channel_id=1, source_target_pairs={{8,0},{16,8},{24,16},{32,24},{40,32},{48,40},{56,48},{64,56},{72,6... | collective-permute-start | bytes 98312 | tf_op jit(solution)/shard_map/ppermute | solution.py:26
  39.2 72.2 %all-to-all-start = ((bf16[64,8,272]{2,0,1:T(8,128)(2,1)}), bf16[64,8,272]{2,0,1:T(8,128)(2,1)S(1)}, u32[]{:S(2)}, u32[]{:S(2)}) async-start(bf16[64,8,272]{2,0,1:T(8,128)(2,1)} %copy.6), calls=%async_computation | async-start | bytes 786432 | tf_op jit(solution)/shard_map/all_to_all | solution.py:95
where the time goes:
time: 113 us; the launch traced here: 112 us
  blocking collectives  57.1 us (51%)
  starting transfers between devices  37.8 us (33%)
  local copies, waits for them, and re-layouts  6.19 us (5%)
  matrix products  5.12 us (5%)
  other arithmetic  5.09 us (5%)
    all_gather x1, blocking collectives, on_device(): frames_all = lax.all_gather(side_tr, 'tm', axis=0, tiled=True)  57.1 us
    ppermute x3, starting transfers between devices, passed_along(): return lax.ppermute(block, axis, route)  13.4 us
    all_to_all x1, starting transfers between devices, on_device(): lax.all_to_all(movie_ext, 'tm', split_axis=1, concat_axis=0, tiled=True)  10.9 us
    ppermute x2, starting transfers between devices, with_halo(): lax.ppermute(head, axis, [((i + 1) % count, i) for i in range(ends)])  9.65 us
    ppermute x2, starting transfers between devices, with_halo(): lax.ppermute(tail, axis, [(i, (i + 1) % count) for i in range(ends)])  3.84 us
    dot_general x7, matrix products, contract_first(): lax.dot_general(left, right, (((0,), (0,)), ((), ())), preferred_element_...  2.64 us
    gather x1, local copies, waits for them, and re-layouts, on_device(): diag_own = jnp.diagonal(gram_own) + 1e-06  2.34 us
    gather x1, local copies, waits for them, and re-layouts, on_device(): divisor = jnp.maximum(jnp.diagonal(q_own), 1.0)  2.34 us
  transfers between devices with their start and end apart: 8, of which 0 were waited for; matrix products, arithmetic and copies ran while one was open for 10% of the time, Pallas kernels for 0%

commit v1 on v0

--- a/solution.py
+++ b/solution.py
@@ -82,7 +82,10 @@
     new_tr = lax.fori_loop(0, GROUPS_DEV, sweep, start_tr)
     rounded = new_tr.astype(jnp.bfloat16)
     side_tr = with_halo(rounded, (("slab", 1),), neurons)
-    frames_all = lax.all_gather(side_tr, "tm", axis=0, tiled=True)
+    n_dev = lax.axis_size("tm")
+    parts = jnp.stack([side_tr for _ in range(n_dev)])
+    parts = lax.all_to_all(parts, "tm", split_axis=0, concat_axis=0)
+    frames_all = jnp.concatenate(parts, axis=0)
     prev_all = frames_all[:, :neurons]
     own_all = frames_all[:, neurons : 2 * neurons]
     next_all = frames_all[:, 2 * neurons :]

time: 113 us -> 97.5 us (0.86)
  blocking collectives: 57.1 us -> 0 us
  waiting for transfers between devices: 0.03 us -> 37.2 us
  starting transfers between devices: 37.8 us -> 39.9 us
  local copies, waits for them, and re-layouts: 6.19 us -> 7.86 us
    all_gather x1 -> x0, blocking collectives: 57.1 us -> none  [on_device(): frames_all = lax.all_gather(side_tr, 'tm', axis=0, tiled=True)]
    all_to_all x0 -> x1, waiting for transfers between devices: none -> 20 us  [on_device(): parts = lax.all_to_all(parts, 'tm', split_axis=0, concat_axis=0)]
    all_to_all x1, waiting for transfers between devices: 0.01 us -> 11.8 us  [on_device(): lax.all_to_all(movie_ext, 'tm', split_axis=1, concat_axis=0, tiled=True)]
    all_to_all x0 -> x1, starting transfers between devices: none -> 10.9 us  [on_device(): parts = lax.all_to_all(parts, 'tm', split_axis=0, concat_axis=0)]
    all_to_all x1, starting transfers between devices: 10.9 us -> 3.45 us  [on_device(): lax.all_to_all(movie_ext, 'tm', split_axis=1, concat_axis=0, tiled=True)]
    ppermute x2, waiting for transfers between devices: 0.01 us -> 5.41 us  [with_halo(): lax.ppermute(tail, axis, [(i, (i + 1) % count) for i in range(ends)])]
    ppermute x2, starting transfers between devices: 9.65 us -> 8.3 us  [with_halo(): lax.ppermute(head, axis, [((i + 1) % count, i) for i in range(ends)])]
  transfers between devices with their start and end apart: 8 -> 9, of which waited for: 0 -> 3; matrix products, arithmetic and copies ran while one was open for 10% -> 10% of each run, Pallas kernels for 0% -> 0%
where the time goes in v1:
time: 97.5 us; the launch traced here: 96.9 us
  starting transfers between devices  39.9 us (41%)
  waiting for transfers between devices  37.2 us (38%)
  local copies, waits for them, and re-layouts  7.86 us (8%)
  matrix products  5.85 us (6%)
  other arithmetic  5.09 us (5%)
    all_to_all x1, waiting for transfers between devices, on_device(): parts = lax.all_to_all(parts, 'tm', split_axis=0, concat_axis=0)  20 us
    ppermute x3, starting transfers between devices, passed_along(): return lax.ppermute(block, axis, route)  13.4 us
    all_to_all x1, waiting for transfers between devices, on_device(): lax.all_to_all(movie_ext, 'tm', split_axis=1, concat_axis=0, tiled=True)  11.8 us
    all_to_all x1, starting transfers between devices, on_device(): parts = lax.all_to_all(parts, 'tm', split_axis=0, concat_axis=0)  10.9 us
    ppermute x2, starting transfers between devices, with_halo(): lax.ppermute(head, axis, [((i + 1) % count, i) for i in range(ends)])  8.3 us
    ppermute x2, waiting for transfers between devices, with_halo(): lax.ppermute(tail, axis, [(i, (i + 1) % count) for i in range(ends)])  5.41 us
    ppermute x2, starting transfers between devices, with_halo(): lax.ppermute(tail, axis, [(i, (i + 1) % count) for i in range(ends)])  3.84 us
    all_to_all x1, starting transfers between devices, on_device(): lax.all_to_all(movie_ext, 'tm', split_axis=1, concat_axis=0, tiled=True)  3.45 us
  transfers between devices with their start and end apart: 9, of which 3 were waited for; matrix products, arithmetic and copies ran while one was open for 10% of the time, Pallas kernels for 0%

profile of v1, /device:TPU:32, one launch (start us, length us, event | category | flops | bytes accessed | tf_op | source)
XLA Modules:
  0.0 96.9 jit_solution(12130789898216621821)
XLA Ops:
  0.6 1.3 %fusion.28 = s32[]{:T(128)} fusion(s32[32]{0:T(128)} %param.9, s32[]{:T(128)S(6)} %axis_index.23), kind=kLoop, calls=%fused_computation.46 | loop fusion | flops 95 | bytes 136 | tf_op jit(solution)/shard_map/reduce_sum | solution.py:47
  1.9 0.6 iota_compare_fusion.1
  2.6 0.8 broadcast_select_fusion
  3.4 3.9 %collective-permute-start.3 = (f32[64,256]{1,0:T(8,128)S(1)}, f32[64,256]{1,0:T(8,128)S(1)}, u32[]{:S(2)}, u32[]{:S(2)}) collective-permute-start(f32[64,256]{1,0:T(8,128)S(1)} %broadcast_select_fusion), channel_id=1, source_target_pairs={{8,0},{16,8},{24,16},{32,24},{40,32},{48,40},{56,48},{64,56},{72,6... | collective-permute-start | bytes 196616 | tf_op jit(solution)/shard_map/ppermute | solution.py:26
  7.3 1.9 %collective-permute-start.1 = (f32[64,256]{1,0:T(8,128)S(1)}, f32[64,256]{1,0:T(8,128)S(1)}, u32[]{:S(2)}, u32[]{:S(2)}) collective-permute-start(f32[64,256]{1,0:T(8,128)S(1)} %broadcast_select_fusion), channel_id=1, source_target_pairs={{0,8},{8,16},{16,24},{24,32},{32,40},{40,48},{48,56},{56,64},{64,7... | collective-permute-start | bytes 196616 | tf_op jit(solution)/shard_map/ppermute | solution.py:24
  9.3 0.7 slice.20
  10.0 5.7 %collective-permute-start = (bf16[64,128]{1,0:T(8,128)(2,1)S(1)}, bf16[64,128]{1,0:T(8,128)(2,1)S(1)}, u32[]{:S(2)}, u32[]{:S(2)}) collective-permute-start(bf16[64,128]{1,0:T(8,128)(2,1)S(1)} %slice.20), channel_id=1, source_target_pairs={{8,0},{16,8},{24,16},{32,24},{40,32},{48,40},{56,48},{64,56},{72,6... | collective-permute-start | bytes 49160 | tf_op jit(solution)/shard_map/ppermute | solution.py:13
  15.8 0.0 copy-start.1
  15.8 2.3 %and_select_fusion = bf16[2176,256]{1,0:T(8,128)(2,1)S(1)} fusion(bf16[2176,256]{1,0:T(8,128)(2,1)} %param.7, pred[256]{0:T(512)(128)(4,1)S(1)} %iota_compare_fusion.1, pred[2176]{0:T(1024)(128)(4,1)S(1)} %fusion.24), kind=kLoop, calls=%fused_computation.11 | loop fusion | flops 1114112 | bytes 2230656 | tf_op jit(solution)/shard_map/jit(_where)/select_n | solution.py:51
  18.1 1.9 %collective-permute-start.2 = (bf16[128,256]{1,0:T(8,128)(2,1)S(1)}, bf16[128,256]{1,0:T(8,128)(2,1)S(1)}, u32[]{:S(2)}, u32[]{:S(2)}) collective-permute-start(bf16[128,256]{1,0:T(8,128)(2,1)S(1)} %get-tuple-element.124), channel_id=1, source_target_pairs={{0,8},{8,16},{16,24},{24,32},{32,40},{40,48},{48,56},{56,64},{64,7... | collective-permute-start | bytes 196616 | tf_op jit(solution)/shard_map/ppermute | solution.py:13
  20.0 5.8 %collective-permute-start.4 = (bf16[128,256]{1,0:T(8,128)(2,1)S(1)}, bf16[128,256]{1,0:T(8,128)(2,1)S(1)}, u32[]{:S(2)}, u32[]{:S(2)}) collective-permute-start(bf16[128,256]{1,0:T(8,128)(2,1)S(1)} %get-tuple-element.125), channel_id=1, source_target_pairs={{8,0},{16,8},{24,16},{32,24},{40,32},{48,40},{56,48},{64,56},{72,6... | collective-permute-start | bytes 196616 | tf_op jit(solution)/shard_map/ppermute | solution.py:13
  25.8 0.5 fusion.37
  26.3 2.3 %gather_fusion = f32[256]{0:T(256)S(1)} fusion(f32[256,256]{1,0:T(8,128)S(1)} %fusion.37, s32[256]{0:T(256)S(1)} %bitcast.36), kind=kCustom, calls=%fused_computation | custom fusion | bytes 4096 | tf_op jit(solution)/shard_map/jit(diagonal)/cond/branch_0_fun/gather | solution.py:62
  28.7 0.0 collective-permute-done
  28.7 0.3 fusion.36
  29.0 0.0 collective-permute-done.4
  29.0 0.2 fusion.31
  29.2 0.0 collective-permute-done.2
  29.2 0.2 fusion.33
  29.5 0.0 collective-permute-done.3
  29.5 0.4 fusion.38
  29.8 0.0 collective-permute-done.1
  29.8 0.4 convolution_add_fusion.2
  30.2 0.7 while.13
  30.2 0.1 dynamic_slice.68
  30.3 0.2 fusion.59
  30.6 0.1 dynamic_slice.68
  30.6 0.2 fusion.59
  30.9 0.0 copy-start
  30.9 4.4 %collective-permute-start.6 = (bf16[64,256]{1,0:T(8,128)(2,1)S(1)}, bf16[64,256]{1,0:T(8,128)(2,1)S(1)}, u32[]{:S(2)}, u32[]{:S(2)}) collective-permute-start(bf16[64,256]{1,0:T(8,128)(2,1)S(1)} %convert_element_type.12), channel_id=1, source_target_pairs={{8,0},{16,8},{24,16},{32,24},{40,32},{48,40},{56,48},{64,56},{72,6... | collective-permute-start | bytes 98312 | tf_op jit(solution)/shard_map/ppermute | solution.py:26
  35.3 1.9 %collective-permute-start.5 = (bf16[64,256]{1,0:T(8,128)(2,1)S(1)}, bf16[64,256]{1,0:T(8,128)(2,1)S(1)}, u32[]{:S(2)}, u32[]{:S(2)}) collective-permute-start(bf16[64,256]{1,0:T(8,128)(2,1)S(1)} %convert_element_type.12), channel_id=1, source_target_pairs={{0,8},{8,16},{16,24},{24,32},{32,40},{40,48},{48,56},{56,64},{64,7... | collective-permute-start | bytes 98312 | tf_op jit(solution)/shard_map/ppermute | solution.py:24
  37.3 0.0 collective-permute-done.6
  37.3 5.4 %collective-permute-done.5 = bf16[64,256]{1,0:T(8,128)(2,1)S(1)} collective-permute-done((bf16[64,256]{1,0:T(8,128)(2,1)S(1)}, bf16[64,256]{1,0:T(8,128)(2,1)S(1)}, u32[]{:S(2)}, u32[]{:S(2)}) %collective-permute-start.5) | collective-permute-done | bytes 32800 | tf_op jit(solution)/shard_map/ppermute | solution.py:24
  42.7 1.0 stack.2
  43.7 10.9 %all-to-all-start.1 = ((bf16[8,64,768]{2,1,0:T(8,128)(2,1)}), bf16[8,64,768]{2,1,0:T(8,128)(2,1)S(1)}, u32[]{:S(2)}, u32[]{:S(2)}) async-start(bf16[8,64,768]{2,1,0:T(8,128)(2,1)} %stack.2), calls=%async_computation.1 | async-start | bytes 1572864 | tf_op jit(solution)/shard_map/all_to_all | solution.py:87
  54.6 0.5 all_to_all.17
  55.1 0.8 copy.6
  55.9 20.0 %all-to-all-done.1 = bf16[8,64,768]{2,1,0:T(8,128)(2,1)S(1)} async-done(((bf16[8,64,768]{2,1,0:T(8,128)(2,1)}), bf16[8,64,768]{2,1,0:T(8,128)(2,1)S(1)}, u32[]{:S(2)}, u32[]{:S(2)}) %all-to-all-start.1) | async-done | bytes 786464 | tf_op jit(solution)/shard_map/all_to_all | solution.py:87
  75.8 3.5 %all-to-all-start = ((bf16[64,8,272]{2,0,1:T(8,128)(2,1)}), bf16[64,8,272]{2,0,1:T(8,128)(2,1)S(1)}, u32[]{:S(2)}, u32[]{:S(2)}) async-start(bf16[64,8,272]{2,0,1:T(8,128)(2,1)} %copy.6), calls=%async_computation | async-start | bytes 786432 | tf_op jit(solution)/shard_map/all_to_all | solution.py:98
  79.3 0.3 fusion.18
  79.6 1.0 fusion.12
  80.5 0.3 fusion.14
  80.8 11.8 %all-to-all-done = bf16[64,8,272]{2,0,1:T(8,128)(2,1)S(1)} async-done(((bf16[64,8,272]{2,0,1:T(8,128)(2,1)}), bf16[64,8,272]{2,0,1:T(8,128)(2,1)S(1)}, u32[]{:S(2)}, u32[]{:S(2)}) %all-to-all-start) | async-done | bytes 278560 | tf_op jit(solution)/shard_map/all_to_all | solution.py:98
  92.6 0.3 fusion.20
  92.9 2.3 %gather_fusion.1 = f32[256]{0:T(256)S(1)} fusion(f32[256,256]{1,0:T(8,128)S(1)} %fusion.18, s32[256]{0:T(256)S(1)} %bitcast.37), kind=kCustom, calls=%fused_computation.1 | custom fusion | bytes 4096 | tf_op jit(solution)/shard_map/jit(diagonal)/cond/branch_0_fun/gather | solution.py:95
  95.2 0.3 fusion.22
  95.6 0.3 convolution_add_fusion.1
  95.9 1.0 %fusion.11 = bf16[272,256]{1,0:T(8,128)(2,1)} fusion(f32[272,256]{1,0:T(8,128)S(1)} %fusion.20, f32[272,256]{1,0:T(8,128)S(1)} %convolution_add_fusion.1, f32[256,256]{1,0:T(8,128)S(1)} %copy-done.2, s32[]{:T(128)S(6)} %select_n.38, bf16[128,256]{1,0:T(8,128)(2,1)S(1)} %collective-permute-done.4, f32[256]{0:T(256)S(1)} %broadcast_maximum_fusion, ...), kind=kOutput, calls=%fused_computation.18 | convolution fusion | flops 214396928 | bytes 1165312 | tf_op jit(solution)/shard_map/dot_general | solution.py:108
  (15 shorter events, 0.1 us)
Async XLA Ops:
  3.4 26.0 %collective-permute-start.3 = (f32[64,256]{1,0:T(8,128)S(1)}, f32[64,256]{1,0:T(8,128)S(1)}, u32[]{:S(2)}, u32[]{:S(2)}) collective-permute-start(f32[64,256]{1,0:T(8,128)S(1)} %broadcast_select_fusion), channel_id=1, source_target_pairs={{8,0},{16,8},{24,16},{32,24},{40,32},{48,40},{56,48},{64,56},{72,6... | collective-permute-start | bytes 196616 | tf_op jit(solution)/shard_map/ppermute | solution.py:26
  7.3 22.5 %collective-permute-start.1 = (f32[64,256]{1,0:T(8,128)S(1)}, f32[64,256]{1,0:T(8,128)S(1)}, u32[]{:S(2)}, u32[]{:S(2)}) collective-permute-start(f32[64,256]{1,0:T(8,128)S(1)} %broadcast_select_fusion), channel_id=1, source_target_pairs={{0,8},{8,16},{16,24},{24,32},{32,40},{40,48},{48,56},{56,64},{64,7... | collective-permute-start | bytes 196616 | tf_op jit(solution)/shard_map/ppermute | solution.py:24
  10.0 18.7 %collective-permute-start = (bf16[64,128]{1,0:T(8,128)(2,1)S(1)}, bf16[64,128]{1,0:T(8,128)(2,1)S(1)}, u32[]{:S(2)}, u32[]{:S(2)}) collective-permute-start(bf16[64,128]{1,0:T(8,128)(2,1)S(1)} %slice.20), channel_id=1, source_target_pairs={{8,0},{16,8},{24,16},{32,24},{40,32},{48,40},{56,48},{64,56},{72,6... | collective-permute-start | bytes 49160 | tf_op jit(solution)/shard_map/ppermute | solution.py:13
  15.8 10.0 %copy-start.1 = (bf16[64,2048]{1,0:T(8,128)(2,1)S(1)}, bf16[64,2048]{1,0:T(8,128)(2,1)}, u32[]{:S(2)}) copy-start(bf16[64,2048]{1,0:T(8,128)(2,1)} %param.6) | copy-start | bytes 786436
  18.1 11.2 %collective-permute-start.2 = (bf16[128,256]{1,0:T(8,128)(2,1)S(1)}, bf16[128,256]{1,0:T(8,128)(2,1)S(1)}, u32[]{:S(2)}, u32[]{:S(2)}) collective-permute-start(bf16[128,256]{1,0:T(8,128)(2,1)S(1)} %get-tuple-element.124), channel_id=1, source_target_pairs={{0,8},{8,16},{16,24},{24,32},{32,40},{40,48},{48,56},{56,64},{64,7... | collective-permute-start | bytes 196616 | tf_op jit(solution)/shard_map/ppermute | solution.py:13
  20.0 9.0 %collective-permute-start.4 = (bf16[128,256]{1,0:T(8,128)(2,1)S(1)}, bf16[128,256]{1,0:T(8,128)(2,1)S(1)}, u32[]{:S(2)}, u32[]{:S(2)}) collective-permute-start(bf16[128,256]{1,0:T(8,128)(2,1)S(1)} %get-tuple-element.125), channel_id=1, source_target_pairs={{8,0},{16,8},{24,16},{32,24},{40,32},{48,40},{56,48},{64,56},{72,6... | collective-permute-start | bytes 196616 | tf_op jit(solution)/shard_map/ppermute | solution.py:13
  30.9 12.8 %copy-start = (f32[64,256]{1,0:T(8,128)}, f32[64,256]{1,0:T(8,128)S(1)}, u32[]{:S(2)}) copy-start(f32[64,256]{1,0:T(8,128)S(1)} %get-tuple-element.109) | copy-start | bytes 196612
  30.9 6.3 %collective-permute-start.6 = (bf16[64,256]{1,0:T(8,128)(2,1)S(1)}, bf16[64,256]{1,0:T(8,128)(2,1)S(1)}, u32[]{:S(2)}, u32[]{:S(2)}) collective-permute-start(bf16[64,256]{1,0:T(8,128)(2,1)S(1)} %convert_element_type.12), channel_id=1, source_target_pairs={{8,0},{16,8},{24,16},{32,24},{40,32},{48,40},{56,48},{64,56},{72,6... | collective-permute-start | bytes 98312 | tf_op jit(solution)/shard_map/ppermute | solution.py:26
  35.3 7.3 %collective-permute-start.5 = (bf16[64,256]{1,0:T(8,128)(2,1)S(1)}, bf16[64,256]{1,0:T(8,128)(2,1)S(1)}, u32[]{:S(2)}, u32[]{:S(2)}) collective-permute-start(bf16[64,256]{1,0:T(8,128)(2,1)S(1)} %convert_element_type.12), channel_id=1, source_target_pairs={{0,8},{8,16},{16,24},{24,32},{32,40},{40,48},{48,56},{56,64},{64,7... | collective-permute-start | bytes 98312 | tf_op jit(solution)/shard_map/ppermute | solution.py:24
  43.7 32.2 %all-to-all-start.1 = ((bf16[8,64,768]{2,1,0:T(8,128)(2,1)}), bf16[8,64,768]{2,1,0:T(8,128)(2,1)S(1)}, u32[]{:S(2)}, u32[]{:S(2)}) async-start(bf16[8,64,768]{2,1,0:T(8,128)(2,1)} %stack.2), calls=%async_computation.1 | async-start | bytes 1572864 | tf_op jit(solution)/shard_map/all_to_all | solution.py:87
  75.8 16.7 %all-to-all-start = ((bf16[64,8,272]{2,0,1:T(8,128)(2,1)}), bf16[64,8,272]{2,0,1:T(8,128)(2,1)S(1)}, u32[]{:S(2)}, u32[]{:S(2)}) async-start(bf16[64,8,272]{2,0,1:T(8,128)(2,1)} %copy.6), calls=%async_computation | async-start | bytes 786432 | tf_op jit(solution)/shard_map/all_to_all | solution.py:98
  92.9 3.0 %copy-start.2 = (f32[256,256]{1,0:T(8,128)S(1)}, f32[256,256]{1,0:T(8,128)}, u32[]{:S(2)}) copy-start(f32[256,256]{1,0:T(8,128)} %fusion.12) | copy-start | bytes 786436
